TPU v7x, 512 devices: a whole 4x8x8 slice. The times are simulated.
512 devices in a mesh: field: 32 (over x, y), cap: 4 (over z_lo, core), bank: 4 (over z_hi).
Axes of the slice: x: 4, y: 8, z: 8 (z_hi: 4, z_lo: 2; z = z_hi * 2 + z_lo), core: 2. Of those that a mesh axis runs over, the one named last changes fastest.
Arguments:
- pattern: bfloat16 [4, 3, 542, 8192], P('cap', None, None, 'field'), may hold values from -6 to 6
- measured: bfloat16 [4, 3, 32, 8192], P('cap', None, None, 'field'), may hold values from -6 to 6
- row_kernels: bfloat16 [64, 3, 16, 511], P('field', None, 'bank'), may hold values from -0.125 to 0.125
- col_kernels: bfloat16 [64, 3, 16, 511], P('field', None, 'bank'), may hold values from -0.125 to 0.125
- tile_patch: int32 [64], P('field'), may hold values from 0 to 1
- sat_tiles: int32 [4, 256], P('cap'), may hold values from 0 to 1023
Outputs:
- grad_rows: float32 [64, 3, 16, 511], P('field', None, 'bank')
- grad_cols: float32 [64, 3, 16, 511], P('field', None, 'bank')
Inputs may be any that keep to these rules, and one draw needn't show every extreme that they name: Patch t of the window uses kernel set (t // 2) * 2 + tile_patch[t]. `sat_tiles`: tile numbers run row by row over tiles of 16 x 16 pixels of the window; an entry may repeat.
All inputs are finite; a program needn't handle non-finite values.
Results may differ from a plain program's by a relative error of at most 0.0033.
Values may be sent and summed in bfloat16 or wider, within the bound.
A program may use at most 64 MiB of HBM per device.

v0:
```python
import jax
import jax.numpy as jnp
from jax import lax
from jax.sharding import PartitionSpec as P

TILE = 16


def with_halo(cells, sides, width):
    for axis, dim in sides:
        count = lax.axis_size(axis)
        ends = count - 1
        head = lax.slice_in_dim(cells, 0, width, axis=dim)
        tail = lax.slice_in_dim(cells, cells.shape[dim] - width, cells.shape[dim], axis=dim)
        cells = jnp.concatenate(
            [
                lax.ppermute(tail, axis, [(i, (i + 1) % count) for i in range(ends)]),
                cells,
                lax.ppermute(head, axis, [((i + 1) % count, i) for i in range(ends)]),
            ],
            axis=dim,
        )
    return cells


def banded(kernel, band_width):
    tap_count = kernel.shape[-1]
    span_len = band_width + tap_count - 1
    zero_tail = jnp.zeros(kernel.shape[:-1] + (band_width,), kernel.dtype)
    padded = jnp.concatenate([kernel, zero_tail], axis=-1)
    repeated = jnp.tile(padded, (1,) * (kernel.ndim - 1) + (band_width,))
    return repeated[..., : band_width * span_len].reshape(
        kernel.shape[:-1] + (band_width, span_len)
    )


def diagonals(matrix, tap_count):
    line_count = matrix.shape[-2]
    span_len = matrix.shape[-1]
    flattened = matrix.reshape(matrix.shape[:-2] + (line_count * span_len,))
    lead_len = (line_count - 1) * (span_len + 1)
    shaped = flattened[..., :lead_len].reshape(matrix.shape[:-2] + (line_count - 1, span_len + 1))
    last_line = flattened[..., lead_len : lead_len + tap_count]
    return jnp.sum(shaped[..., :tap_count], axis=-2) + last_line


def body(pattern, measured, row_kernels, col_kernels, tile_patch, sat_tiles):
    captures, colours, rows_ext, strip_width = pattern.shape
    height = measured.shape[2]
    tap_count = row_kernels.shape[-1]
    rim_width = (tap_count - 1) // 2
    tile_count = row_kernels.shape[0]
    patch_width = strip_width // tile_count
    extended = with_halo(pattern, (("field", 3),), rim_width)
    strip_tiles = strip_width // TILE
    across = strip_tiles * lax.axis_size("field")
    row_ids = jnp.arange(height // TILE, dtype=jnp.int32)
    col_ids = lax.axis_index("field") * strip_tiles + jnp.arange(strip_tiles, dtype=jnp.int32)
    tile_ids = row_ids[:, None] * across + col_ids[None, :]
    saturated = jnp.any(tile_ids[None, :, :, None] == sat_tiles[:, None, None, :], axis=-1)
    keep_tiles = 1.0 - saturated.astype(jnp.float32)
    keep_pixels = jnp.broadcast_to(
        keep_tiles[:, :, None, :, None], (captures, height // TILE, TILE, strip_tiles, TILE)
    ).reshape(captures, height, strip_width)
    slots = jnp.arange(tile_count, dtype=jnp.int32)
    selectors = []
    windows = []
    col_bands = []
    rowpasses = []
    partials = []
    for tile_index in range(tile_count):
        selector = (tile_patch[tile_index] == slots).astype(jnp.float32)
        row_taps = jnp.einsum("k,kqrb->qrb", selector, row_kernels.astype(jnp.float32)).astype(
            jnp.bfloat16
        )
        col_taps = jnp.einsum("k,kqrb->qrb", selector, col_kernels.astype(jnp.float32)).astype(
            jnp.bfloat16
        )
        row_band = banded(row_taps, patch_width)
        col_band = banded(col_taps, height)
        start = tile_index * patch_width
        window_cols = extended[..., start : start + patch_width + 2 * rim_width]
        rowpass = jnp.einsum(
            "cqyj,qrxj->cqryx", window_cols, row_band, preferred_element_type=jnp.float32
        ).astype(jnp.bfloat16)
        partial_tile = jnp.einsum(
            "qryk,cqrkx->cqyx", col_band, rowpass, preferred_element_type=jnp.float32
        )
        selectors.append(selector)
        windows.append(window_cols)
        col_bands.append(col_band)
        rowpasses.append(rowpass)
        partials.append(partial_tile)
    partial_value = jnp.concatenate(partials, axis=3)
    predicted = lax.psum(partial_value, "bank")
    residual = (keep_pixels[:, None] * (predicted - measured.astype(jnp.float32))).astype(
        jnp.bfloat16
    )
    rank_count = row_kernels.shape[2]
    row_total = jnp.zeros((tile_count, colours, rank_count, tap_count), jnp.float32)
    col_total = jnp.zeros((tile_count, colours, rank_count, tap_count), jnp.float32)
    for tile_index in range(tile_count):
        start = tile_index * patch_width
        residual_tile = residual[..., start : start + patch_width]
        backward = jnp.einsum(
            "qryk,cqyx->cqrkx",
            col_bands[tile_index],
            residual_tile,
            preferred_element_type=jnp.float32,
        ).astype(jnp.bfloat16)
        row_terms = jnp.einsum(
            "cqrkx,cqkj->qrxj", backward, windows[tile_index], preferred_element_type=jnp.float32
        )
        col_terms = jnp.einsum(
            "cqyx,cqrkx->qryk",
            residual_tile,
            rowpasses[tile_index],
            preferred_element_type=jnp.float32,
        )
        row_grad = diagonals(row_terms, tap_count)
        col_grad = diagonals(col_terms, tap_count)
        row_total = row_total + selectors[tile_index][:, None, None, None] * row_grad[None]
        col_total = col_total + selectors[tile_index][:, None, None, None] * col_grad[None]
    summed_rows, summed_cols = lax.psum((row_total, col_total), "cap")
    return (summed_rows * (1.0 / height), summed_cols * (1.0 / height))


def solution(mesh):
    return jax.shard_map(
        body,
        mesh=mesh,
        in_specs=(
            P("cap", None, None, "field"),
            P("cap", None, None, "field"),
            P("field", None, "bank", None),
            P("field", None, "bank", None),
            P("field"),
            P("cap", None),
        ),
        out_specs=(P("field", None, "bank", None), P("field", None, "bank", None)),
        check_vma=False,
    )
```

profile of v0, /device:TPU:1, one launch (start us, length us, event | category | flops | bytes accessed | tf_op | source)
XLA Modules:
  0.0 245.0 jit_solution(10084475282999751488)
XLA Ops:
  7.3 3.0 %fusion.46 = (bf16[1,3,542,255]{3,2,1,0:T(8,128)(2,1)}, bf16[1,3,542,255]{3,2,1,0:T(8,128)(2,1)}) fusion(bf16[1,3,542,256]{3,2,1,0:T(8,128)(2,1)} %param.6), kind=kLoop, calls=%fused_computation.70 | loop fusion | bytes 3317040 | tf_op jit(solution)/shard_map/slice | solution.py:14
  10.2 4.9 %collective-permute-start = (bf16[1,3,542,255]{3,2,1,0:T(8,128)(2,1)}, bf16[1,3,542,255]{3,2,1,0:T(8,128)(2,1)}, u32[]{:S(2)}, u32[]{:S(2)}) collective-permute-start(bf16[1,3,542,255]{3,2,1,0:T(8,128)(2,1)} %get-tuple-element.4), channel_id=1, source_target_pairs={{0,16},{16,32},{32,48},{48,64},{64,80},{80,96},{96,112},{112,128},... | collective-permute-start | bytes 2487788 | tf_op jit(solution)/shard_map/ppermute | solution.py:17
  24.1 1.6 reshape.178
  25.9 5.4 %tile.41 = bf16[3,4,81792]{2,1,0:T(4,128)(2,1)} reshape(bf16[3,4,128,639]{3,2,1,0:T(8,128)(2,1)S(1)} %tile.40) | data formatting | bytes 3926016 | tf_op jit(solution)/shard_map/tile | solution.py:31
  32.9 5.2 %reshape.179 = bf16[3,4,128,638]{3,2,1,0:T(8,128)(2,1)} reshape(bf16[3,4,81664]{2,1,0:T(4,128)(2,1)S(1)} %slice-done) | data formatting | bytes 3919872 | tf_op jit(solution)/shard_map/reshape | solution.py:32
  38.2 5.3 %tile.17 = bf16[3,4,81792]{2,1,0:T(4,128)(2,1)} reshape(bf16[3,4,128,639]{3,2,1,0:T(8,128)(2,1)S(1)} %tile.16) | data formatting | bytes 3926016 | tf_op jit(solution)/shard_map/tile | solution.py:31
  45.0 5.2 %reshape.175 = bf16[3,4,128,638]{3,2,1,0:T(8,128)(2,1)} reshape(bf16[3,4,81664]{2,1,0:T(4,128)(2,1)S(1)} %slice-done.1) | data formatting | bytes 3919872 | tf_op jit(solution)/shard_map/reshape | solution.py:32
  50.3 2.7 %pad_maximum_fusion = bf16[1,3,542,766]{3,2,1,0:T(8,128)(2,1)S(1)} fusion(bf16[1,3,542,255]{3,2,1,0:T(8,128)(2,1)} %collective-permute-done.1, bf16[1,3,542,256]{3,2,1,0:T(8,128)(2,1)S(1)} %copy-done.2, bf16[1,3,542,255]{3,2,1,0:T(8,128)(2,1)} %collective-permute-done), kind=kLoop, calls=%fused_computation.2 | loop fusion | flops 7473096 | bytes 4982064 | tf_op jit(solution)/shard_map/concatenate | solution.py:15
  60.6 58.8 %all-reduce.8.cloned.1.call-done = f32[1,3,32,256]{3,2,1,0:T(8,128)} async-done(((f32[1,3,32,256]{3,2,1,0:T(8,128)}), f32[1,3,32,256]{3,2,1,0:T(8,128)}) %all-reduce.8.cloned.1.call-update) | async-done | bytes 98320 | tf_op jit(solution)/shard_map/psum | solution.py:95
  120.3 1.7 fusion.19
  122.0 1.7 fusion.16
  123.7 6.2 %fusion.2 = f32[3,4,128,638]{3,2,1,0:T(8,128)} fusion(bf16[1,3,542,766]{3,2,1,0:T(8,128)(2,1)} %copy-done.5, bf16[3,4,32,542]{3,2,1,0:T(8,128)(2,1)S(1)} %copy-done.9, bf16[1,3,32,256]{3,2,1,0:T(8,128)(2,1)S(1)} %multiply_convert_fusion), kind=kOutput, calls=%fused_computation.7 | convolution fusion | flops 1116398592 | bytes 6524928 | tf_op jit(solution)/shard_map/cqrkx,cqkj->qrxj/dot_general | solution.py:111
  129.9 6.3 %fusion = f32[3,4,128,638]{3,2,1,0:T(8,128)} fusion(bf16[1,3,542,766]{3,2,1,0:T(8,128)(2,1)} %copy-done.5, bf16[3,4,32,542]{3,2,1,0:T(8,128)(2,1)S(1)} %copy-done.11, bf16[1,3,32,256]{3,2,1,0:T(8,128)(2,1)S(1)} %multiply_convert_fusion), kind=kOutput, calls=%fused_computation.5 | convolution fusion | flops 1116398592 | bytes 6524928 | tf_op jit(solution)/shard_map/cqrkx,cqkj->qrxj/dot_general | solution.py:111
  138.4 2.0 reshape.194
  141.7 2.0 reshape.192
  145.0 7.2 %reshape.189 = f32[3,4,81664]{2,1,0:T(4,128)} reshape(f32[3,4,128,638]{3,2,1,0:T(8,128)} %fusion.2) | data formatting | bytes 7839744 | tf_op jit(solution)/shard_map/reshape | solution.py:40
  152.2 6.9 %reshape.185 = f32[3,4,81664]{2,1,0:T(4,128)} reshape(f32[3,4,128,638]{3,2,1,0:T(8,128)} %fusion) | data formatting | bytes 7839744 | tf_op jit(solution)/shard_map/reshape | solution.py:40
  159.1 4.3 %slice.103 = f32[3,4,81153]{2,1,0:T(4,128)} slice(f32[3,4,81664]{2,1,0:T(4,128)} %reshape.185), slice={[0:3], [0:4], [0:81153]} | slice | bytes 7790688 | tf_op jit(solution)/shard_map/slice | solution.py:42
  163.4 7.3 %reshape.186 = f32[3,4,127,639]{3,2,1,0:T(8,128)} reshape(f32[3,4,81153]{2,1,0:T(4,128)} %slice.103) | data formatting | bytes 7790688 | tf_op jit(solution)/shard_map/reshape | solution.py:42
  170.6 2.3 slice_reduce_fusion.1
  172.9 4.3 %slice.107 = f32[3,4,81153]{2,1,0:T(4,128)} slice(f32[3,4,81664]{2,1,0:T(4,128)} %reshape.189), slice={[0:3], [0:4], [0:81153]} | slice | bytes 7790688 | tf_op jit(solution)/shard_map/slice | solution.py:42
  177.2 7.3 %reshape.190 = f32[3,4,127,639]{3,2,1,0:T(8,128)} reshape(f32[3,4,81153]{2,1,0:T(4,128)} %slice.107) | data formatting | bytes 7790688 | tf_op jit(solution)/shard_map/reshape | solution.py:42
  184.5 2.3 slice_reduce_fusion
  188.4 46.9 %all-reduce.10.cloned.1.call-done = (f32[2,3,4,511]{3,2,1,0:T(4,128)}, f32[2,3,4,511]{3,2,1,0:T(4,128)}) async-done(((f32[2,3,4,511]{3,2,1,0:T(4,128)}, f32[2,3,4,511]{3,2,1,0:T(4,128)}), (f32[2,3,4,511]{3,2,1,0:T(4,128)}, f32[2,3,4,511]{3,2,1,0:T(4,128)})) %all-reduce.10.cloned.1.call-update) | async-done | bytes 98128 | tf_op jit(solution)/shard_map/psum | solution.py:124
  (88 shorter events, 30.1 us)
Async XLA Ops:
  7.2 9.9 %copy-start = (bf16[2,3,4,511]{3,2,1,0:T(4,128)(2,1)S(1)}, bf16[2,3,4,511]{3,2,1,0:T(4,128)(2,1)}, u32[]{:S(2)}) copy-start(bf16[2,3,4,511]{3,2,1,0:T(4,128)(2,1)} %param.9) | copy-start | bytes 73588
  7.2 9.3 %copy-start.13 = (s32[2]{0:T(128)S(1)}, s32[2]{0:T(128)}, u32[]{:S(2)}) copy-start(s32[2]{0:T(128)} %param.10) | copy-start | bytes 28
  7.2 10.7 %copy-start.15 = (bf16[2,3,4,511]{3,2,1,0:T(4,128)(2,1)S(1)}, bf16[2,3,4,511]{3,2,1,0:T(4,128)(2,1)}, u32[]{:S(2)}) copy-start(bf16[2,3,4,511]{3,2,1,0:T(4,128)(2,1)} %param.8) | copy-start | bytes 73588
  7.2 13.3 %copy-start.14 = (s32[1,256]{1,0:T(1,128)S(1)}, s32[1,256]{1,0:T(1,128)}, u32[]{:S(2)}) copy-start(s32[1,256]{1,0:T(1,128)} %param.11) | copy-start | bytes 3076
  7.2 112.2 %all-reduce.8.cloned.1.call-start = ((), (), s32[]{:S(2)}) async-start(), calls=%async_computation | async-start | bytes 196608 | tf_op jit(solution)/shard_map/psum | solution.py:95
  10.2 40.0 %collective-permute-start = (bf16[1,3,542,255]{3,2,1,0:T(8,128)(2,1)}, bf16[1,3,542,255]{3,2,1,0:T(8,128)(2,1)}, u32[]{:S(2)}, u32[]{:S(2)}) collective-permute-start(bf16[1,3,542,255]{3,2,1,0:T(8,128)(2,1)} %get-tuple-element.4), channel_id=1, source_target_pairs={{0,16},{16,32},{32,48},{48,64},{64,80},{80,96},{96,112},{112,128},... | collective-permute-start | bytes 2487788 | tf_op jit(solution)/shard_map/ppermute | solution.py:17
  15.2 35.1 %collective-permute-start.1 = (bf16[1,3,542,255]{3,2,1,0:T(8,128)(2,1)}, bf16[1,3,542,255]{3,2,1,0:T(8,128)(2,1)}, u32[]{:S(2)}, u32[]{:S(2)}) collective-permute-start(bf16[1,3,542,255]{3,2,1,0:T(8,128)(2,1)} %get-tuple-element.5), channel_id=1, source_target_pairs={{16,0},{32,16},{48,32},{64,48},{80,64},{96,80},{112,96},{128,112},... | collective-permute-start | bytes 2487788 | tf_op jit(solution)/shard_map/ppermute | solution.py:19
  31.3 1.5 slice-start
  43.5 1.5 slice-start.1
  45.0 5.3 %copy-start.2 = (bf16[1,3,542,256]{3,2,1,0:T(8,128)(2,1)S(1)}, bf16[1,3,542,256]{3,2,1,0:T(8,128)(2,1)}, u32[]{:S(2)}) copy-start(bf16[1,3,542,256]{3,2,1,0:T(8,128)(2,1)} %param.6) | copy-start | bytes 2497540
  50.3 2.7 %copy-start.6 = (bf16[3,4,128,638]{3,2,1,0:T(8,128)(2,1)S(1)}, bf16[3,4,128,638]{3,2,1,0:T(8,128)(2,1)}, u32[]{:S(2)}) copy-start(bf16[3,4,128,638]{3,2,1,0:T(8,128)(2,1)} %reshape.179) | copy-start | bytes 5879812
  53.0 1.5 copy-start.5
  53.0 2.5 %copy-start.7 = (bf16[3,4,128,638]{3,2,1,0:T(8,128)(2,1)S(1)}, bf16[3,4,128,638]{3,2,1,0:T(8,128)(2,1)}, u32[]{:S(2)}) copy-start(bf16[3,4,128,638]{3,2,1,0:T(8,128)(2,1)} %reshape.175) | copy-start | bytes 5879812
  55.4 1.5 copy-start.8
  57.0 1.0 copy-start.10
  57.0 62.5 %copy-start.12 = (bf16[1,3,32,256]{3,2,1,0:T(8,128)(2,1)S(1)}, bf16[1,3,32,256]{3,2,1,0:T(8,128)(2,1)}, u32[]{:S(2)}) copy-start(bf16[1,3,32,256]{3,2,1,0:T(8,128)(2,1)} %param.7) | copy-start | bytes 147460
  59.1 176.3 %all-reduce.10.cloned.1.call-start = ((), (), s32[]{:S(2)}) async-start(), calls=%async_computation.1 | async-start | bytes 196608 | tf_op jit(solution)/shard_map/psum | solution.py:124
  122.0 1.7 copy-start.9
  123.7 6.2 %copy-start.11 = (bf16[3,4,32,542]{3,2,1,0:T(8,128)(2,1)S(1)}, bf16[3,4,32,542]{3,2,1,0:T(8,128)(2,1)}, u32[]{:S(2)}) copy-start(bf16[3,4,32,542]{3,2,1,0:T(8,128)(2,1)} %reshape.178) | copy-start | bytes 1248772
  129.9 6.3 %copy-start.4 = (f32[3,4,32,542]{3,2,1,0:T(8,128)S(1)}, f32[3,4,32,542]{3,2,1,0:T(8,128)}, u32[]{:S(2)}) copy-start(f32[3,4,32,542]{3,2,1,0:T(8,128)} %fusion.16) | copy-start | bytes 2497540
  136.2 1.2 copy-start.3
  177.2 61.0 %copy-start.1 = (bf16[2,3,4,511]{3,2,1,0:T(4,128)(2,1)S(1)}, bf16[2,3,4,511]{3,2,1,0:T(4,128)(2,1)}, u32[]{:S(2)}) copy-start(bf16[2,3,4,511]{3,2,1,0:T(4,128)(2,1)} %param.9) | copy-start | bytes 73588
Sparse Core Ops, SparseCore 0:
  59.2 60.1 all-reduce.7
  188.6 46.7 all-reduce.9
where the time goes:
time: 246 us; the launch traced here: 245 us
  waiting for transfers between devices  106 us (43%)
  local copies, waits for them, and re-layouts  78.2 us (32%)
  matrix products  22.8 us (9%)
  other arithmetic  17.4 us (7%)
  between operations  14.4 us (6%)
  starting transfers between devices  6.51 us (3%)
    psum x1, waiting for transfers between devices, body(): predicted = lax.psum(partial_value, 'bank')  58.8 us
    psum x1, waiting for transfers between devices, body(): summed_rows, summed_cols = lax.psum((row_total, col_total), 'cap')  46.9 us
    reshape x4, local copies, waits for them, and re-layouts, diagonals(): flattened[..., :lead_len]  18.5 us
    reshape x4, local copies, waits for them, and re-layouts, diagonals(): flattened = matrix.reshape(matrix.shape[:-2] + (line_count * span_len,))  16.1 us
    reshape x4, local copies, waits for them, and re-layouts, banded(): repeated[..., :band_width * span_len]  13.7 us
    another operation x8, local copies, waits for them, and re-layouts, banded(): repeated = jnp.tile(padded, (1,) * (kernel.ndim - 1) + (band_width,))  12.5 us
    dot_general x2, matrix products, body(): jnp.einsum('cqrkx,cqkj->qrxj', backward, windows[tile_index], preferred_e...  12.5 us
    slice x4, local copies, waits for them, and re-layouts, diagonals(): flattened[..., :lead_len]  8.63 us
  transfers between devices with their start and end apart: 4, of which 2 were waited for; matrix products, arithmetic and copies ran while one was open for 13% of the time, Pallas kernels for 0%

commit v1 on v0

--- a/solution.py
+++ b/solution.py
@@ -92,7 +92,7 @@
         rowpasses.append(rowpass)
         partials.append(partial_tile)
     partial_value = jnp.concatenate(partials, axis=3)
-    predicted = lax.psum(partial_value, "bank")
+    predicted = jnp.sum(lax.all_gather(partial_value, "bank"), axis=0)
     residual = (keep_pixels[:, None] * (predicted - measured.astype(jnp.float32))).astype(
         jnp.bfloat16
     )

time: 246 us -> 211 us (0.86)
  waiting for transfers between devices: 106 us -> 50.8 us
  blocking collectives: 0 us -> 19.6 us
    psum x1 -> x0, waiting for transfers between devices: 58.8 us -> none  [body(): predicted = lax.psum(partial_value, 'bank')]
    all_gather x0 -> x1, blocking collectives: none -> 19.6 us  [body(): predicted = jnp.sum(lax.all_gather(partial_value, 'bank'), axis=0)]
    psum x1, waiting for transfers between devices: 46.9 us -> 50.7 us  [body(): summed_rows, summed_cols = lax.psum((row_total, col_total), 'cap')]
  transfers between devices with their start and end apart: 4 -> 3, of which waited for: 2 -> 1; matrix products, arithmetic and copies ran while one was open for 13% -> 15% of each run, Pallas kernels for 0% -> 0%
where the time goes in v1:
time: 211 us; the launch traced here: 210 us
  local copies, waits for them, and re-layouts  78.3 us (37%)
  waiting for transfers between devices  50.8 us (24%)
  matrix products  22.8 us (11%)
  blocking collectives  19.6 us (9%)
  other arithmetic  17.7 us (8%)
  between operations  14.4 us (7%)
  starting transfers between devices  6.24 us (3%)
    psum x1, waiting for transfers between devices, body(): summed_rows, summed_cols = lax.psum((row_total, col_total), 'cap')  50.7 us
    all_gather x1, blocking collectives, body(): predicted = jnp.sum(lax.all_gather(partial_value, 'bank'), axis=0)  19.6 us
    reshape x4, local copies, waits for them, and re-layouts, diagonals(): flattened[..., :lead_len]  18.6 us
    reshape x4, local copies, waits for them, and re-layouts, diagonals(): flattened = matrix.reshape(matrix.shape[:-2] + (line_count * span_len,))  16.1 us
    reshape x4, local copies, waits for them, and re-layouts, banded(): repeated[..., :band_width * span_len]  13.7 us
    another operation x8, local copies, waits for them, and re-layouts, banded(): repeated = jnp.tile(padded, (1,) * (kernel.ndim - 1) + (band_width,))  12.5 us
    dot_general x2, matrix products, body(): jnp.einsum('cqrkx,cqkj->qrxj', backward, windows[tile_index], preferred_e...  12.5 us
    slice x4, local copies, waits for them, and re-layouts, diagonals(): flattened[..., :lead_len]  8.66 us
  transfers between devices with their start and end apart: 3, of which 1 were waited for; matrix products, arithmetic and copies ran while one was open for 15% of the time, Pallas kernels for 0%

profile of v1, /device:TPU:1, one launch (start us, length us, event | category | flops | bytes accessed | tf_op | source)
XLA Modules:
  0.0 209.8 jit_solution(3562486619929966770)
XLA Ops:
  7.3 3.0 %fusion.48 = (bf16[1,3,542,255]{3,2,1,0:T(8,128)(2,1)}, bf16[1,3,542,255]{3,2,1,0:T(8,128)(2,1)}) fusion(bf16[1,3,542,256]{3,2,1,0:T(8,128)(2,1)} %param.6), kind=kLoop, calls=%fused_computation.72 | loop fusion | bytes 3317040 | tf_op jit(solution)/shard_map/slice | solution.py:14
  10.3 4.9 %collective-permute-start = (bf16[1,3,542,255]{3,2,1,0:T(8,128)(2,1)}, bf16[1,3,542,255]{3,2,1,0:T(8,128)(2,1)}, u32[]{:S(2)}, u32[]{:S(2)}) collective-permute-start(bf16[1,3,542,255]{3,2,1,0:T(8,128)(2,1)} %get-tuple-element.4), channel_id=1, source_target_pairs={{0,16},{16,32},{32,48},{48,64},{64,80},{80,96},{96,112},{112,128},... | collective-permute-start | bytes 2487788 | tf_op jit(solution)/shard_map/ppermute | solution.py:17
  24.2 1.6 reshape.179
  25.9 5.4 %tile.41 = bf16[3,4,81792]{2,1,0:T(4,128)(2,1)} reshape(bf16[3,4,128,639]{3,2,1,0:T(8,128)(2,1)S(1)} %tile.40) | data formatting | bytes 3926016 | tf_op jit(solution)/shard_map/tile | solution.py:31
  32.9 5.2 %reshape.180 = bf16[3,4,128,638]{3,2,1,0:T(8,128)(2,1)} reshape(bf16[3,4,81664]{2,1,0:T(4,128)(2,1)S(1)} %slice-done) | data formatting | bytes 3919872 | tf_op jit(solution)/shard_map/reshape | solution.py:32
  38.2 5.3 %tile.17 = bf16[3,4,81792]{2,1,0:T(4,128)(2,1)} reshape(bf16[3,4,128,639]{3,2,1,0:T(8,128)(2,1)S(1)} %tile.16) | data formatting | bytes 3926016 | tf_op jit(solution)/shard_map/tile | solution.py:31
  45.0 5.2 %reshape.176 = bf16[3,4,128,638]{3,2,1,0:T(8,128)(2,1)} reshape(bf16[3,4,81664]{2,1,0:T(4,128)(2,1)S(1)} %slice-done.1) | data formatting | bytes 3919872 | tf_op jit(solution)/shard_map/reshape | solution.py:32
  51.6 2.7 %pad_maximum_fusion = bf16[1,3,542,766]{3,2,1,0:T(8,128)(2,1)S(1)} fusion(bf16[1,3,542,255]{3,2,1,0:T(8,128)(2,1)} %collective-permute-done.1, bf16[1,3,542,256]{3,2,1,0:T(8,128)(2,1)S(1)} %copy-done.2, bf16[1,3,542,255]{3,2,1,0:T(8,128)(2,1)} %collective-permute-done), kind=kLoop, calls=%fused_computation.2 | loop fusion | flops 7473096 | bytes 4982064 | tf_op jit(solution)/shard_map/concatenate | solution.py:15
  59.7 19.6 %all-gather = f32[4,3,32,256]{3,2,1,0:T(8,128)} all-gather(f32[1,3,32,256]{3,2,1,0:T(8,128)S(1)} %pad_maximum_fusion.1), channel_id=2, replica_groups=mesh['field'=32,'cap'=4,'bank'=4] {'bank'}, dimensions={0}, use_global_device_ids=true | all-gather | bytes 491520 | tf_op jit(solution)/shard_map/all_gather | solution.py:95
  81.2 1.7 fusion.19
  82.9 1.7 fusion.16
  84.6 6.2 %fusion.2 = f32[3,4,128,638]{3,2,1,0:T(8,128)} fusion(bf16[1,3,542,766]{3,2,1,0:T(8,128)(2,1)} %copy-done.5, bf16[3,4,32,542]{3,2,1,0:T(8,128)(2,1)S(1)} %copy-done.9, bf16[1,3,32,256]{3,2,1,0:T(8,128)(2,1)S(1)} %fusion.29), kind=kOutput, calls=%fused_computation.7 | convolution fusion | flops 1116398592 | bytes 6524928 | tf_op jit(solution)/shard_map/cqrkx,cqkj->qrxj/dot_general | solution.py:111
  90.8 6.3 %fusion = f32[3,4,128,638]{3,2,1,0:T(8,128)} fusion(bf16[1,3,542,766]{3,2,1,0:T(8,128)(2,1)} %copy-done.5, bf16[3,4,32,542]{3,2,1,0:T(8,128)(2,1)S(1)} %copy-done.11, bf16[1,3,32,256]{3,2,1,0:T(8,128)(2,1)S(1)} %fusion.29), kind=kOutput, calls=%fused_computation.5 | convolution fusion | flops 1116398592 | bytes 6524928 | tf_op jit(solution)/shard_map/cqrkx,cqkj->qrxj/dot_general | solution.py:111
  99.3 2.0 reshape.195
  102.6 2.0 reshape.193
  105.8 7.2 %reshape.190 = f32[3,4,81664]{2,1,0:T(4,128)} reshape(f32[3,4,128,638]{3,2,1,0:T(8,128)} %fusion.2) | data formatting | bytes 7839744 | tf_op jit(solution)/shard_map/reshape | solution.py:40
  113.0 6.9 %reshape.186 = f32[3,4,81664]{2,1,0:T(4,128)} reshape(f32[3,4,128,638]{3,2,1,0:T(8,128)} %fusion) | data formatting | bytes 7839744 | tf_op jit(solution)/shard_map/reshape | solution.py:40
  120.0 4.3 %slice.103 = f32[3,4,81153]{2,1,0:T(4,128)} slice(f32[3,4,81664]{2,1,0:T(4,128)} %reshape.186), slice={[0:3], [0:4], [0:81153]} | slice | bytes 7790688 | tf_op jit(solution)/shard_map/slice | solution.py:42
  124.2 7.3 %reshape.187 = f32[3,4,127,639]{3,2,1,0:T(8,128)} reshape(f32[3,4,81153]{2,1,0:T(4,128)} %slice.103) | data formatting | bytes 7790688 | tf_op jit(solution)/shard_map/reshape | solution.py:42
  131.5 2.3 %slice_reduce_fusion.1 = f32[3,4,511]{2,1,0:T(4,128)S(1)} fusion(f32[3,4,127,639]{3,2,1,0:T(8,128)} %reshape.187), kind=kLoop, calls=%fused_computation.1 | loop fusion | flops 772632 | bytes 3139584 | tf_op jit(solution)/shard_map/reduce_sum | solution.py:44
  133.8 4.3 %slice.107 = f32[3,4,81153]{2,1,0:T(4,128)} slice(f32[3,4,81664]{2,1,0:T(4,128)} %reshape.190), slice={[0:3], [0:4], [0:81153]} | slice | bytes 7790688 | tf_op jit(solution)/shard_map/slice | solution.py:42
  138.1 7.3 %reshape.191 = f32[3,4,127,639]{3,2,1,0:T(8,128)} reshape(f32[3,4,81153]{2,1,0:T(4,128)} %slice.107) | data formatting | bytes 7790688 | tf_op jit(solution)/shard_map/reshape | solution.py:42
  145.4 2.3 %slice_reduce_fusion = f32[3,4,511]{2,1,0:T(4,128)S(1)} fusion(f32[3,4,127,639]{3,2,1,0:T(8,128)} %reshape.191), kind=kLoop, calls=%fused_computation | loop fusion | flops 772632 | bytes 3139584 | tf_op jit(solution)/shard_map/reduce_sum | solution.py:44
  149.4 50.7 %all-reduce.7.cloned.1.call-done = (f32[2,3,4,511]{3,2,1,0:T(4,128)}, f32[2,3,4,511]{3,2,1,0:T(4,128)}) async-done(((f32[2,3,4,511]{3,2,1,0:T(4,128)}, f32[2,3,4,511]{3,2,1,0:T(4,128)}), (f32[2,3,4,511]{3,2,1,0:T(4,128)}, f32[2,3,4,511]{3,2,1,0:T(4,128)})) %all-reduce.7.cloned.1.call-update) | async-done | bytes 98128 | tf_op jit(solution)/shard_map/psum | solution.py:124
  (85 shorter events, 30.1 us)
Async XLA Ops:
  7.2 9.9 %copy-start = (bf16[2,3,4,511]{3,2,1,0:T(4,128)(2,1)S(1)}, bf16[2,3,4,511]{3,2,1,0:T(4,128)(2,1)}, u32[]{:S(2)}) copy-start(bf16[2,3,4,511]{3,2,1,0:T(4,128)(2,1)} %param.9) | copy-start | bytes 73588
  7.2 9.3 %copy-start.12 = (s32[2]{0:T(128)S(1)}, s32[2]{0:T(128)}, u32[]{:S(2)}) copy-start(s32[2]{0:T(128)} %param.10) | copy-start | bytes 28
  7.2 10.7 %copy-start.14 = (bf16[2,3,4,511]{3,2,1,0:T(4,128)(2,1)S(1)}, bf16[2,3,4,511]{3,2,1,0:T(4,128)(2,1)}, u32[]{:S(2)}) copy-start(bf16[2,3,4,511]{3,2,1,0:T(4,128)(2,1)} %param.8) | copy-start | bytes 73588
  7.2 13.3 %copy-start.13 = (s32[1,256]{1,0:T(1,128)S(1)}, s32[1,256]{1,0:T(1,128)}, u32[]{:S(2)}) copy-start(s32[1,256]{1,0:T(1,128)} %param.11) | copy-start | bytes 3076
  7.2 192.9 %all-reduce.7.cloned.1.call-start = ((), (), s32[]{:S(2)}) async-start(), calls=%async_computation | async-start | bytes 196608 | tf_op jit(solution)/shard_map/psum | solution.py:124
  10.3 41.3 %collective-permute-start = (bf16[1,3,542,255]{3,2,1,0:T(8,128)(2,1)}, bf16[1,3,542,255]{3,2,1,0:T(8,128)(2,1)}, u32[]{:S(2)}, u32[]{:S(2)}) collective-permute-start(bf16[1,3,542,255]{3,2,1,0:T(8,128)(2,1)} %get-tuple-element.4), channel_id=1, source_target_pairs={{0,16},{16,32},{32,48},{48,64},{64,80},{80,96},{96,112},{112,128},... | collective-permute-start | bytes 2487788 | tf_op jit(solution)/shard_map/ppermute | solution.py:17
  15.2 36.4 %collective-permute-start.1 = (bf16[1,3,542,255]{3,2,1,0:T(8,128)(2,1)}, bf16[1,3,542,255]{3,2,1,0:T(8,128)(2,1)}, u32[]{:S(2)}, u32[]{:S(2)}) collective-permute-start(bf16[1,3,542,255]{3,2,1,0:T(8,128)(2,1)} %get-tuple-element.5), channel_id=1, source_target_pairs={{16,0},{32,16},{48,32},{64,48},{80,64},{96,80},{112,96},{128,112},... | collective-permute-start | bytes 2487788 | tf_op jit(solution)/shard_map/ppermute | solution.py:19
  31.3 1.5 slice-start
  43.5 1.5 slice-start.1
  45.0 6.6 %copy-start.2 = (bf16[1,3,542,256]{3,2,1,0:T(8,128)(2,1)S(1)}, bf16[1,3,542,256]{3,2,1,0:T(8,128)(2,1)}, u32[]{:S(2)}) copy-start(bf16[1,3,542,256]{3,2,1,0:T(8,128)(2,1)} %param.6) | copy-start | bytes 2497540
  51.6 2.7 %copy-start.6 = (bf16[3,4,128,638]{3,2,1,0:T(8,128)(2,1)S(1)}, bf16[3,4,128,638]{3,2,1,0:T(8,128)(2,1)}, u32[]{:S(2)}) copy-start(bf16[3,4,128,638]{3,2,1,0:T(8,128)(2,1)} %reshape.180) | copy-start | bytes 5879812
  54.3 1.5 copy-start.5
  54.3 2.5 %copy-start.7 = (bf16[3,4,128,638]{3,2,1,0:T(8,128)(2,1)S(1)}, bf16[3,4,128,638]{3,2,1,0:T(8,128)(2,1)}, u32[]{:S(2)}) copy-start(bf16[3,4,128,638]{3,2,1,0:T(8,128)(2,1)} %reshape.176) | copy-start | bytes 5879812
  56.8 1.5 copy-start.8
  58.3 1.0 copy-start.10
  82.9 1.7 copy-start.9
  84.6 6.2 %copy-start.11 = (bf16[3,4,32,542]{3,2,1,0:T(8,128)(2,1)S(1)}, bf16[3,4,32,542]{3,2,1,0:T(8,128)(2,1)}, u32[]{:S(2)}) copy-start(bf16[3,4,32,542]{3,2,1,0:T(8,128)(2,1)} %reshape.179) | copy-start | bytes 1248772
  90.8 6.3 %copy-start.4 = (f32[3,4,32,542]{3,2,1,0:T(8,128)S(1)}, f32[3,4,32,542]{3,2,1,0:T(8,128)}, u32[]{:S(2)}) copy-start(f32[3,4,32,542]{3,2,1,0:T(8,128)} %fusion.16) | copy-start | bytes 2497540
  97.1 1.2 copy-start.3
  138.1 64.9 %copy-start.1 = (bf16[2,3,4,511]{3,2,1,0:T(4,128)(2,1)S(1)}, bf16[2,3,4,511]{3,2,1,0:T(4,128)(2,1)}, u32[]{:S(2)}) copy-start(bf16[2,3,4,511]{3,2,1,0:T(4,128)(2,1)} %param.9) | copy-start | bytes 73588
Sparse Core Ops, SparseCore 0:
  149.5 50.5 all-reduce.6
